TPU v7x, 32 devices: a whole 2x2x4 slice. The times are simulated.
32 devices in a mesh: ctx: 8 (over y, x, core), head: 4 (over z).
Axes of the slice: x: 2, y: 2, z: 4, core: 2. Of those that a mesh axis runs over, the one named last changes fastest.
Arguments:
- queries: bfloat16 [2048, 4096], P('ctx', 'head'), may hold values from -6 to 6
- keys_values: bfloat16 [2048, 1024], P('ctx'), may hold values from -6 to 6
- grad_rows: bfloat16 [2048, 2880], P('ctx', 'head'), may hold values from -6 to 6
- doc_ids: int32 [2048], replicated, may hold values from 0 to 7, never falling along the last dimension, each value on 1 to 512 neighbouring positions
- tile_list: int32 [16], replicated, may hold values from 0 to 15, each once
Outputs:
- attended: float32 [2048, 4096], P('ctx', 'head')
- weight_grad: float32 [2880, 4096], P('ctx', 'head')
Inputs may be any that keep to these rules, and one draw needn't show every extreme that they name: `tile_list`: every slot index names a different tile. `doc_ids`: never falling along the window; each document holds 1 to 512 positions.
All inputs are finite; a program needn't handle non-finite values.
Results may differ from a plain program's by a relative error of at most 0.0018.
Values may be sent and summed in bfloat16 or wider, within the bound.
A program may use at most 128 MiB of HBM per device.

v0:
```python
import jax
import jax.numpy as jnp
from jax import lax
from jax.sharding import PartitionSpec as P

H = 64
KVH = 8
DH = 64
TILE = 128


NEG_FILL = -1e30


def on_device(queries, keys_values, grad_rows, doc_ids, tile_list):
    tokens_local = queries.shape[0]
    heads_local = queries.shape[1] // DH
    group = H // KVH
    kv_local = max(1, heads_local // group)
    per_kv = heads_local // kv_local
    scale = DH ** (-0.5)
    head_index = lax.axis_index("head")
    kv_start = head_index * heads_local // group
    own_kv = lax.dynamic_slice_in_dim(keys_values, kv_start * 2 * DH, kv_local * 2 * DH, 1)
    tile_count = tile_list.shape[0]
    offsets = jnp.arange(TILE, dtype=jnp.int32)
    slot_pos = (tile_list[:, None] * TILE + offsets[None, :]).reshape(-1)
    slot_doc = doc_ids.reshape(tile_count, TILE)[tile_list].reshape(-1)
    row_start = lax.axis_index("ctx") * tokens_local
    query_pos = lax.dynamic_slice_in_dim(slot_pos, row_start, tokens_local)
    query_doc = lax.dynamic_slice_in_dim(slot_doc, row_start, tokens_local)
    grouped = queries.reshape(tokens_local, kv_local, per_kv, DH)
    piece = lax.all_gather(own_kv, "ctx", axis=0, tiled=True)
    count = piece.shape[0]
    allowed = (query_doc[:, None] == slot_doc[None, :]) & (slot_pos[None, :] <= query_pos[:, None])
    run_max = jnp.full((kv_local, per_kv, tokens_local), NEG_FILL, jnp.float32)
    parts = piece.reshape(count, kv_local, 2, DH)
    keys = parts[:, :, 0]
    values = parts[:, :, 1]
    scores = jnp.einsum("tgqd,ngd->gqtn", grouped, keys, preferred_element_type=jnp.float32) * scale
    masked = jnp.where(allowed, scores, NEG_FILL)
    new_max = jnp.maximum(run_max, jnp.max(masked, axis=-1))
    weights = jnp.where(allowed, jnp.exp(masked - new_max[..., None]), 0.0)
    new_sum = jnp.sum(weights, axis=-1)
    added = jnp.einsum(
        "gqtn,ngd->gqtd", weights.astype(jnp.bfloat16), values, preferred_element_type=jnp.float32
    )
    normed = added / new_sum[..., None]
    attended = jnp.transpose(normed, (2, 0, 1, 3)).reshape(tokens_local, heads_local * DH)
    term = lax.dot_general(
        lax.all_gather(grad_rows, "head", axis=1, tiled=True).astype(jnp.float32),
        attended,
        (((0,), (0,)), ((), ())),
        precision=lax.Precision.HIGHEST,
        preferred_element_type=jnp.float32,
    )
    weight_grad = lax.psum_scatter(term, "ctx", scatter_dimension=0, tiled=True)
    return (attended, weight_grad)


def solution(mesh):
    in_specs = (P("ctx", "head"), P("ctx", None), P("ctx", "head"), P(), P())
    out_specs = (P("ctx", "head"), P("ctx", "head"))
    return jax.shard_map(
        on_device, mesh=mesh, in_specs=in_specs, out_specs=out_specs, check_vma=False
    )
```

profile of v0, /device:TPU:0, one launch (start us, length us, event | category | flops | bytes accessed | tf_op | source)
XLA Modules:
  0.0 184.8 jit_solution(14846848199935776259)
XLA Ops:
  7.2 0.0 copy-start
  7.2 0.0 all-gather.3.cloned.1.call-start
  7.2 1.0 copy-done
  8.2 0.8 copy.19
  9.0 0.0 all-gather.3.cloned.1.call-update
  9.0 0.0 all-gather.5.cloned.1.call-start
  9.1 0.7 all-gather.5.cloned.1.call-update
  9.8 0.0 reduce-scatter.2.cloned.1.call-start
  9.8 0.7 compare_select_fusion
  10.5 0.1 add_bitcast_fusion
  10.6 1.3 gather_fusion
  11.8 0.1 dynamic_slice.9
  11.9 0.1 dynamic_slice.10
  12.0 1.2 copy.12
  13.2 1.4 compare_and_fusion
  14.7 22.1 %all-gather.3.cloned.1.call-done = bf16[2048,256]{0,1:T(8,128)(2,1)} async-done(((bf16[256,256]{0,1:T(8,128)(2,1)}), bf16[2048,256]{0,1:T(8,128)(2,1)}) %all-gather.3.cloned.1.call-update) | async-done | bytes 1048592 | tf_op jit(solution)/shard_map/all_gather | solution.py:33
  36.8 0.0 copy-start.1
  36.8 14.8 %fusion = (f32[2,8,256]{2,1,0:T(8,128)S(1)}, f32[2,2048,256,8]{2,1,3,0:T(8,128)}) fusion(pred[256,2048]{0,1:T(8,128)(4,1)S(1)} %compare_and_fusion, bf16[256,2,8,64]{0,3,2,1:T(8,128)(2,1)S(1)} %bitcast.52, bf16[2048,2,2,64]{0,3,2,1:T(8,128)(2,1)} %bitcast.54), kind=kOutput, calls=%fused_computation.3 | convolution fusion | flops 1098903552 | bytes 35143680 | tf_op jit(solution)/shard_map/tgqd,ngd->gqtn/dot_general | solution.py:40
  51.6 14.9 %fusion.1 = f32[2,8,256]{2,1,0:T(8,128)S(1)} fusion(f32[2,2048,256,8]{2,1,3,0:T(8,128)} %get-tuple-element.9, f32[2,8,256]{2,1,0:T(8,128)S(1)} %broadcast_maximum_fusion, pred[256,2048]{0,1:T(8,128)(4,1)S(1)} %compare_and_fusion), kind=kLoop, calls=%fused_computation.4 | loop fusion | flops 41938944 | bytes 34111488 | tf_op jit(solution)/shard_map/reduce_sum | solution.py:44
  66.5 0.0 copy-done.1
  66.6 14.3 %fusion.9 = f32[256,2,8,64]{0,3,2,1:T(8,128)S(1)} fusion(f32[2,2048,256,8]{2,1,3,0:T(8,128)} %get-tuple-element.9, f32[2,8,256]{2,1,0:T(8,128)S(1)} %broadcast_maximum_fusion, pred[256,2048]{0,1:T(8,128)(4,1)S(1)} %compare_and_fusion, bf16[2048,2,2,64]{0,3,2,1:T(8,128)(2,1)S(1)} %bitcast.55, f32[256,2,8]{0,2,1:T(8,128)S(1)} %bitcast.58), kind=kOutput, calls=%fused_computation.11 | convolution fusion | flops 1115947008 | bytes 35684352 | tf_op jit(solution)/shard_map/gqtn,ngd->gqtd/dot_general | solution.py:45
  80.9 0.0 all-gather.5.cloned.1.call-done
  80.9 9.0 %convolution_bitcast_fusion = f32[2880,1024]{1,0:T(8,128)} fusion(f32[256,1024]{0,1:T(8,128)S(1)} %bitcast.50, bf16[256,2880]{0,1:T(8,128)(2,1)} %all-gather.5.cloned.1.call-done), kind=kOutput, calls=%fused_computation.8 | convolution fusion | flops 9059696640 | bytes 14319616 | tf_op jit(solution)/shard_map/dot_general | solution.py:50
  89.9 0.0 reduce-scatter.2.cloned.1.call-update
  89.9 1.3 copy.15
  91.2 87.0 %reduce-scatter.2.cloned.1.call-done = f32[360,1024]{1,0:T(8,128)} async-done(((f32[2880,1024]{1,0:T(8,128)}), f32[360,1024]{1,0:T(8,128)}) %reduce-scatter.2.cloned.1.call-update) | async-done | bytes 1474576 | tf_op jit(solution)/shard_map/reduce_scatter | solution.py:57
  (3 shorter events, 0.0 us)
Async XLA Ops:
  7.2 1.0 copy-start
  7.2 29.6 %all-gather.3.cloned.1.call-start = ((), (), s32[]{:S(2)}) async-start(), calls=%async_computation.1 | async-start | bytes 1179648 | tf_op jit(solution)/shard_map/all_gather | solution.py:33
  9.0 71.9 %all-gather.5.cloned.1.call-start = ((), (), s32[]{:S(2)}) async-start(), calls=%async_computation.2 | async-start | bytes 1843200 | tf_op jit(solution)/shard_map/all_gather | solution.py:51
  9.8 168.5 %reduce-scatter.2.cloned.1.call-start = ((), (), s32[]{:S(2)}) async-start(), calls=%async_computation.3 | async-start | bytes 13271040 | tf_op jit(solution)/shard_map/reduce_scatter | solution.py:57
  36.8 29.8 %copy-start.1 = (bf16[2048,256]{0,1:T(8,128)(2,1)S(1)}, bf16[2048,256]{0,1:T(8,128)(2,1)}, u32[]{:S(2)}) copy-start(bf16[2048,256]{0,1:T(8,128)(2,1)} %all-gather.3.cloned.1.call-done) | copy-start | bytes 3145732
Sparse Core Ops, SparseCore 0:
  10.5 26.2 all-gather.2
  38.3 35.4 all-gather.4
  90.0 88.1 reduce-scatter.1
where the time goes:
time: 185 us
  waiting for transfers between devices  110 us (59%)
  matrix products  38.1 us (21%)
  other arithmetic  17.1 us (9%)
  between operations  13.8 us (7%)
  local copies, waits for them, and re-layouts  5.72 us (3%)
    reduce_scatter x1, waiting for transfers between devices, on_device(): weight_grad = lax.psum_scatter(term, 'ctx', scatter_dimension=0, tiled=True)  87 us
    all_gather x1, waiting for transfers between devices, on_device(): piece = lax.all_gather(own_kv, 'ctx', axis=0, tiled=True)  22.1 us
    reduce_sum x1, other arithmetic, on_device(): new_sum = jnp.sum(weights, axis=-1)  14.9 us
    dot_general x1, matrix products, on_device(): jnp.einsum('tgqd,ngd->gqtn', grouped, keys, preferred_element_type=jnp.fl...  14.8 us
    dot_general x1, matrix products, on_device(): jnp.einsum('gqtn,ngd->gqtd', weights.astype(jnp.bfloat16), values, prefer...  14.3 us
    dot_general x1, matrix products, on_device(): lax.dot_general(lax.all_gather(grad_rows, 'head', axis=1, tiled=True).ast...  9.01 us
    unnamed x7, local copies, waits for them, and re-layouts  4.29 us
  transfers between devices with their start and end apart: 3, of which 2 were waited for; matrix products, arithmetic and copies ran while one was open for 27% of the time, Pallas kernels for 0%

commit v1 on v0

v1 whole, which is shorter than its diff:
```python
import functools
import jax
import jax.numpy as jnp
from jax import lax
from jax.experimental import pallas as pl
from jax.experimental.pallas import tpu as pltpu
from jax.sharding import PartitionSpec as P

H = 64
KVH = 8
DH = 64
TILE = 128

NEG_FILL = -1e30


def attend_kernel(pairs, lo_ref, hi_ref, slot_ref, q_ref, kv_ref, start_ref, pos_ref,
                  out_ref, low_ref, s_ref, m_ref, l_ref, o_ref):
    t = pl.program_id(0)
    lo = lo_ref[t]
    hi = hi_ref[t]
    lane = lax.broadcasted_iota(jnp.int32, (TILE, TILE), 1)
    first = lane < DH
    q = jnp.concatenate(
        [q_ref[:, 2 * DH * i:2 * DH * (i + 1)] for i in range(pairs)], axis=0
    ) * jnp.bfloat16(DH ** -0.5)
    start = start_ref[...]
    pos = pos_ref[...]

    def tile_of(p):
        kv = kv_ref[pl.ds(pl.multiple_of(slot_ref[p] * TILE, TILE), TILE), :].astype(jnp.float32)
        return kv, pltpu.roll(kv, DH, 1)

    m_ref[...] = jnp.full_like(m_ref, NEG_FILL)

    @pl.loop(lo, hi + 1)
    def _(p):
        kv, swapped = tile_of(p)
        keys = jnp.concatenate(
            [jnp.where(first, kv, 0.0), jnp.where(first, 0.0, swapped)], axis=0
        ).astype(jnp.bfloat16)
        s = lax.dot_general(q, keys, (((1,), (1,)), ((), ())), preferred_element_type=jnp.float32)
        at = p * TILE + lane
        bias = jnp.where((at >= start) & (at <= pos), 0.0, NEG_FILL)
        bias = jnp.concatenate([bias, bias], axis=1)
        s = s + jnp.concatenate([bias] * pairs, axis=0)
        s_ref[p - lo] = s
        m_ref[...] = jnp.maximum(m_ref[...], s)

    m_even = jnp.max(m_ref[:, :TILE], axis=1, keepdims=True)
    m_odd = jnp.max(m_ref[:, TILE:], axis=1, keepdims=True)
    m_ref[:, :TILE] = jnp.broadcast_to(m_even, (pairs * TILE, TILE))
    m_ref[:, TILE:] = jnp.broadcast_to(m_odd, (pairs * TILE, TILE))
    l_ref[...] = jnp.zeros_like(l_ref)
    o_ref[...] = jnp.zeros_like(o_ref)

    @pl.loop(lo, hi + 1)
    def _(p):
        kv, swapped = tile_of(p)
        values = jnp.concatenate(
            [jnp.where(first, swapped, 0.0), jnp.where(first, 0.0, kv)], axis=0
        ).astype(jnp.bfloat16)
        w = jnp.exp(s_ref[p - lo] - m_ref[...])
        l_ref[...] += w
        o_ref[...] += jnp.dot(w.astype(jnp.bfloat16), values, preferred_element_type=jnp.float32)

    l_even = jnp.sum(l_ref[:, :TILE], axis=1, keepdims=True)
    l_odd = jnp.sum(l_ref[:, TILE:], axis=1, keepdims=True)
    wide = lax.broadcasted_iota(jnp.int32, (pairs * TILE, TILE), 1)
    o = o_ref[...] / jnp.where(wide < DH, l_even, l_odd)
    for i in range(pairs):
        part = o[i * TILE:(i + 1) * TILE]
        out_ref[:, 2 * DH * i:2 * DH * (i + 1)] = part
        low_ref[:, 2 * DH * i:2 * DH * (i + 1)] = part.astype(jnp.bfloat16)


def attend(queries, kv, lo, hi, slot, start, pos, kv_local, per_kv):
    rows, width = queries.shape
    keys = kv.shape[0]
    pairs = per_kv // 2
    block = pl.BlockSpec((TILE, per_kv * DH), lambda t, g, *_: (t, g))
    column = pl.BlockSpec((TILE, 1), lambda t, g, *_: (t, 0))
    stack = pairs * TILE
    scores_bytes = keys // TILE * stack * 2 * TILE * 4
    return pl.pallas_call(
        functools.partial(attend_kernel, pairs),
        grid_spec=pltpu.PrefetchScalarGridSpec(
            num_scalar_prefetch=3,
            grid=(rows // TILE, kv_local),
            in_specs=[block, pl.BlockSpec((keys, 2 * DH), lambda t, g, *_: (0, g)), column, column],
            out_specs=[block, block],
            scratch_shapes=[
                pltpu.VMEM((keys // TILE, stack, 2 * TILE), jnp.float32),
                pltpu.VMEM((stack, 2 * TILE), jnp.float32),
                pltpu.VMEM((stack, 2 * TILE), jnp.float32),
                pltpu.VMEM((stack, TILE), jnp.float32),
            ],
        ),
        out_shape=[
            jax.ShapeDtypeStruct((rows, width), jnp.float32),
            jax.ShapeDtypeStruct((rows, width), jnp.bfloat16),
        ],
        compiler_params=pltpu.CompilerParams(vmem_limit_bytes=scores_bytes + (16 << 20)),
        cost_estimate=pl.CostEstimate(
            flops=rows * width * keys, bytes_accessed=rows * width * 8 + keys * 512,
            transcendentals=rows * width * keys // DH // 4,
        ),
    )(lo, hi, slot, queries, kv, start, pos)


def on_device(queries, keys_values, grad_rows, doc_ids, tile_list):
    tokens_local = queries.shape[0]
    heads_local = queries.shape[1] // DH
    group = H // KVH
    kv_local = max(1, heads_local // group)
    per_kv = heads_local // kv_local
    kv_start = lax.axis_index("head") * heads_local // group
    own_kv = lax.dynamic_slice_in_dim(keys_values, kv_start * 2 * DH, kv_local * 2 * DH, 1)
    kv = lax.all_gather(own_kv, "ctx", axis=0, tiled=True)

    tile_count = tile_list.shape[0]
    tiles_local = tokens_local // TILE
    numbers = jnp.arange(tile_count, dtype=jnp.int32)
    slot = jnp.sum(jnp.where(tile_list[None, :] == numbers[:, None], numbers[None, :], 0), axis=1, dtype=jnp.int32)
    hi = lax.dynamic_slice_in_dim(tile_list, lax.axis_index("ctx") * tiles_local, tiles_local)
    docs = doc_ids.reshape(tile_count, TILE)[hi]
    start = jnp.sum(doc_ids[None, None, :] < docs[:, :, None], axis=2, dtype=jnp.int32)
    pos = hi[:, None] * TILE + jnp.arange(TILE, dtype=jnp.int32)[None, :]
    lo = start[:, 0] // TILE

    attended, low = attend(
        queries, kv, lo, hi, slot, start.reshape(-1, 1), pos.reshape(-1, 1), kv_local, per_kv
    )
    grads = lax.all_gather(grad_rows, "head", axis=1, tiled=True)
    grads = lax.all_to_all(grads, "ctx", split_axis=1, concat_axis=0, tiled=True)
    low_all = lax.all_gather(low, "ctx", axis=0, tiled=True)
    weight_grad = lax.dot_general(
        grads, low_all, (((0,), (0,)), ((), ())), preferred_element_type=jnp.float32
    )
    return (attended, weight_grad)


def solution(mesh):
    in_specs = (P("ctx", "head"), P("ctx", None), P("ctx", "head"), P(), P())
    out_specs = (P("ctx", "head"), P("ctx", "head"))
    return jax.shard_map(
        on_device, mesh=mesh, in_specs=in_specs, out_specs=out_specs, check_vma=False
    )
```

time: 185 us -> 133 us (0.72)
  waiting for transfers between devices: 110 us -> 60.9 us
  matrix products: 38.1 us -> 4.98 us
  blocking collectives: 0 us -> 29.2 us
  Pallas kernels: 0 us -> 14.8 us
  other arithmetic: 17.1 us -> 2.65 us
    reduce_scatter x1 -> x0, waiting for transfers between devices: 87 us -> none  [on_device(): weight_grad = lax.psum_scatter(term, 'ctx', scatter_dimension=0, tiled=True)]
    all_gather x2 -> x3, waiting for transfers between devices: 22.1 us -> 60.2 us  [the longest x1 22.7 us: on_device(): kv = lax.all_gather(own_kv, 'ctx', axis=0, tiled=True)]
    dot_general x3 -> x1, matrix products: 38.1 us -> 4.98 us  [on_device(): lax.dot_general(grads, low_all, (((0,), (0,)), ((), ())), preferred_eleme...]
    all_to_all x0 -> x1, blocking collectives: none -> 29.2 us  [on_device(): lax.all_to_all(grads, 'ctx', split_axis=1, concat_axis=0, tiled=True)]
    pallas_call x0 -> x1, Pallas kernels: none -> 14.8 us  [attend(): pl.pallas_call(functools.partial(attend_kernel, pairs), grid_spec=pltpu.P...]
    reduce_sum x1 -> x2, other arithmetic: 14.9 us -> 1.82 us  [the longest x1 1.04 us: on_device(): jnp.sum(doc_ids[None, None, :] < docs[:, :, None], axis=2, dtype=jnp.int32)]
    unnamed x7 -> x6, local copies, waits for them, and re-layouts: 4.29 us -> 3.24 us
  transfers between devices with their start and end apart: 3 -> 3, of which waited for: 2 -> 3; matrix products, arithmetic and copies ran while one was open for 27% -> 3% of each run, Pallas kernels for 0% -> 11%
where the time goes in v1:
time: 133 us; the launch traced here: 132 us
  waiting for transfers between devices  60.9 us (46%)
  blocking collectives  29.2 us (22%)
  Pallas kernels  14.8 us (11%)
  between operations  13.8 us (10%)
  local copies, waits for them, and re-layouts  5.74 us (4%)
  matrix products  4.98 us (4%)
  other arithmetic  2.65 us (2%)
    all_to_all x1, blocking collectives, on_device(): lax.all_to_all(grads, 'ctx', split_axis=1, concat_axis=0, tiled=True)  29.2 us
    all_gather x1, waiting for transfers between devices, on_device(): kv = lax.all_gather(own_kv, 'ctx', axis=0, tiled=True)  22.7 us
    all_gather x1, waiting for transfers between devices, on_device(): grads = lax.all_gather(grad_rows, 'head', axis=1, tiled=True)  20 us
    all_gather x1, waiting for transfers between devices, on_device(): low_all = lax.all_gather(low, 'ctx', axis=0, tiled=True)  17.5 us
    pallas_call x1, Pallas kernels, attend(): pl.pallas_call(functools.partial(attend_kernel, pairs), grid_spec=pltpu.P...  14.8 us
    dot_general x1, matrix products, on_device(): lax.dot_general(grads, low_all, (((0,), (0,)), ((), ())), preferred_eleme...  4.98 us
    unnamed x6, local copies, waits for them, and re-layouts  3.24 us
  transfers between devices with their start and end apart: 3, of which 3 were waited for; matrix products, arithmetic and copies ran while one was open for 3% of the time, Pallas kernels for 11%

profile of v1, /device:TPU:0, one launch (start us, length us, event | category | flops | bytes accessed | tf_op | source)
XLA Modules:
  0.0 132.2 jit_solution(6275284867218926931)
XLA Ops:
  7.2 0.0 copy-start
  7.2 0.0 all-gather.4.cloned.1.call-start
  7.2 1.0 copy-done
  8.2 0.7 constant_dynamic-slice_fusion
  8.9 0.0 all-gather.4.cloned.1.call-update
  8.9 0.0 all-gather.8.cloned.1.call-start
  9.0 0.7 all-gather.8.cloned.1.call-update
  9.7 0.0 all-gather.6.cloned.1.call-start
  9.7 0.7 broadcast_multiply_fusion
  10.4 0.1 iota_add_fusion
  10.5 0.1 copy.18.pos_ref
  10.7 1.3 gather_fusion
  11.9 1.0 convert_reduce_fusion
  13.0 0.1 copy.17.start_ref
  13.1 0.1 slice_reduce_fusion
  13.3 0.8 select_reduce_fusion.slot_ref
  14.0 22.7 %all-gather.4.cloned.1.call-done.kv_ref = bf16[2048,256]{1,0:T(8,128)(2,1)} async-done(((bf16[256,256]{1,0:T(8,128)(2,1)}), bf16[2048,256]{1,0:T(8,128)(2,1)}) %all-gather.4.cloned.1.call-update) | async-done | bytes 1048592 | tf_op jit(solution)/shard_map/all_gather | solution.py:119
  36.7 0.0 copy-start.1
  36.7 1.2 copy-done.1
  37.9 0.0 copy-start.2
  37.9 1.0 copy-done.2
  39.0 14.8 %shard_map.68 = (f32[256,1024]{1,0:T(8,128)}, bf16[256,1024]{1,0:T(8,128)(2,1)}) custom-call(s32[2]{0:T(128)S(1)} %and_select_fusion.lo_ref, s32[2]{0:T(128)S(1)} %get-tuple-element.7.hi_ref, s32[16]{0:T(128)S(1)} %select_reduce_fusion.slot_ref, bf16[256,1024]{1,0:T(8,128)(2,1)S(1)} %copy-done.2, bf16[2048,256]{1,0:T(8,128)(2,1)S(1)} %copy-done.1, ...), custom_call_target="tpu_custom_call" | custom-call | flops 536870912 | bytes 3145728 | tf_op jit(solution)/shard_map/pallas_call | solution.py:85
  53.7 0.0 all-gather.6.cloned.1.call-update
  53.8 20.0 %all-gather.8.cloned.1.call-done = bf16[256,2880]{0,1:T(8,128)(2,1)} async-done(((bf16[256,720]{0,1:T(8,128)(2,1)}), bf16[256,2880]{0,1:T(8,128)(2,1)}) %all-gather.8.cloned.1.call-update) | async-done | bytes 1474576 | tf_op jit(solution)/shard_map/all_gather | solution.py:134
  73.8 29.2 %all_to_all.19 = bf16[256,8,360]{0,2,1:T(8,128)(2,1)S(1)} all-to-all(bf16[256,8,360]{0,2,1:T(8,128)(2,1)} %bitcast.12), channel_id=1, replica_groups=mesh['ctx'=8,'head'=4] {'ctx'}, dimensions={1} | all-to-all | bytes 2949120 | tf_op jit(solution)/shard_map/all_to_all | solution.py:135
  103.0 0.2 copy.20
  103.2 17.5 %all-gather.6.cloned.1.call-done = bf16[2048,1024]{1,0:T(8,128)(2,1)} async-done(((bf16[256,1024]{1,0:T(8,128)(2,1)}), bf16[2048,1024]{1,0:T(8,128)(2,1)}) %all-gather.6.cloned.1.call-update) | async-done | bytes 4194320 | tf_op jit(solution)/shard_map/all_gather | solution.py:136
  120.7 5.0 %convolution_bitcast_fusion = f32[360,1024]{1,0:T(8,128)} fusion(bf16[2048,1024]{1,0:T(8,128)(2,1)} %all-gather.6.cloned.1.call-done, bf16[2048,360]{0,1:T(8,128)(2,1)S(1)} %bitcast.13), kind=kOutput, calls=%fused_computation.2 | convolution fusion | flops 1509949440 | bytes 7143424 | tf_op jit(solution)/shard_map/dot_general | solution.py:137
  (3 shorter events, 0.0 us)
Async XLA Ops:
  7.2 1.0 copy-start
  7.2 29.5 %all-gather.4.cloned.1.call-start = ((), (), s32[]{:S(2)}) async-start(), calls=%async_computation.1 | async-start | bytes 1179648 | tf_op jit(solution)/shard_map/all_gather | solution.py:119
  8.9 64.9 %all-gather.8.cloned.1.call-start = ((), (), s32[]{:S(2)}) async-start(), calls=%async_computation.3 | async-start | bytes 1843200 | tf_op jit(solution)/shard_map/all_gather | solution.py:134
  9.7 111.0 %all-gather.6.cloned.1.call-start = ((), (), s32[]{:S(2)}) async-start(), calls=%async_computation.2 | async-start | bytes 4718592 | tf_op jit(solution)/shard_map/all_gather | solution.py:136
  36.7 1.2 copy-start.1
  37.9 1.0 copy-start.2
Sparse Core Ops, SparseCore 0:
  10.5 26.1 all-gather.3
  38.3 35.4 all-gather.7
  76.3 44.3 all-gather.5

commit v2 on v1

--- a/solution.py
+++ b/solution.py
@@ -12,6 +12,171 @@
 TILE = 128
 
 NEG_FILL = -1e30
+
+MESH = pl.DeviceIdType.MESH
+
+
+def greet(others, head_too):
+    me, n = lax.axis_index("ctx"), others
+    barrier = pltpu.get_barrier_semaphore()
+    for j in range(1, n):
+        pl.semaphore_signal(barrier, inc=1, device_id={"ctx": lax.rem(me + j, n)}, device_id_type=MESH)
+    for j in range(1, head_too):
+        to = lax.rem(lax.axis_index("head") + j, head_too)
+        pl.semaphore_signal(barrier, inc=1, device_id={"head": to}, device_id_type=MESH)
+    pl.semaphore_wait(barrier, n - 1 + max(0, head_too - 1))
+
+
+class Gather:
+    def __init__(self, src, slots, send, recv, own):
+        self.n = n = slots.shape[0]
+        self.half = half = n // 2
+        self.me = me = lax.axis_index("ctx")
+        self.pair, self.side = me // 2, me % 2
+        self.mate = self.pair * 2 + 1 - self.side
+        self.slots, self.send, self.recv = slots, send, recv
+        self.local = pltpu.make_async_copy(src, slots.at[me], own)
+        self.sends = [
+            self.copy(src, me, lax.rem(self.pair + j, half) * 2 + self.side, j - 1) for j in range(1, half)
+        ]
+        self.sends.append(self.copy(src, me, self.mate, half - 1))
+
+    def copy(self, src, owner, to, i):
+        return pltpu.make_async_remote_copy(
+            src_ref=src, dst_ref=self.slots.at[owner], send_sem=self.send.at[i],
+            recv_sem=self.recv.at[owner], device_id={"ctx": to}, device_id_type=MESH,
+        )
+
+    def start(self):
+        for c in self.sends:
+            c.start()
+        self.local.start()
+
+    def forward(self, j):
+        owner = lax.rem(self.pair + self.half - j, self.half) * 2 + self.side
+        c = self.copy(self.slots.at[owner], owner, self.mate, self.half - 1 + j)
+        c.wait_recv()
+        c.start()
+        self.sends.append(c)
+
+    def finish(self):
+        self.local.wait()
+        for j in range(self.half):
+            owner = lax.rem(self.pair + self.half - j, self.half) * 2 + 1 - self.side
+            self.copy(self.slots.at[owner], owner, self.mate, 0).wait_recv()
+        for c in self.sends:
+            c.wait_send()
+
+
+def gather_kernel(src_ref, slots_ref, send, recv, own):
+    n = slots_ref.shape[0]
+    greet(n, 0)
+    g = Gather(src_ref, slots_ref, send, recv, own)
+    g.start()
+    for j in range(1, g.half):
+        g.forward(j)
+    g.finish()
+
+
+def gather(x, n):
+    return pl.pallas_call(
+        gather_kernel,
+        out_shape=jax.ShapeDtypeStruct((n,) + x.shape, x.dtype),
+        in_specs=[pl.BlockSpec(memory_space=pl.ANY)],
+        out_specs=pl.BlockSpec(memory_space=pl.ANY),
+        scratch_shapes=[
+            pltpu.SemaphoreType.DMA((n - 1,)), pltpu.SemaphoreType.DMA((n,)), pltpu.SemaphoreType.DMA,
+        ],
+        compiler_params=pltpu.CompilerParams(collective_id=0, has_side_effects=True),
+    )(x)
+
+
+def grad_kernel(low_ref, g_ref, out_ref, att, spread, terms, send, recv, own,
+                z_send, z_recv, z_own, a_send, a_recv, a_own):
+    n, heads, halves = att.shape[0], spread.shape[0], spread.shape[1]
+    me, head = lax.axis_index("ctx"), lax.axis_index("head")
+    greet(n, heads)
+
+    z_copies = [
+        pltpu.make_async_remote_copy(
+            src_ref=g_ref, dst_ref=spread.at[d], send_sem=z_send.at[d], recv_sem=z_recv.at[d],
+            device_id={"head": lax.rem(head + d, heads)}, device_id_type=MESH,
+        )
+        for d in range(1, heads)
+    ]
+    for c in z_copies:
+        c.start()
+    z_local = pltpu.make_async_copy(g_ref, spread.at[0], z_own)
+    z_local.start()
+    g = Gather(low_ref, att, send, recv, own)
+    g.start()
+
+    def block(src, to):
+        return pltpu.make_async_remote_copy(
+            src_ref=src, dst_ref=terms.at[me], send_sem=a_send.at[to], recv_sem=a_recv.at[me],
+            device_id={"ctx": to}, device_id_type=MESH,
+        )
+
+    def hand_out(d):
+        for k in range(halves):
+            to = lax.rem(head + heads - d, heads) * halves + k
+
+            @pl.when(to != me)
+            def _():
+                block(spread.at[d, k], to).start()
+
+            @pl.when(to == me)
+            def _():
+                pltpu.make_async_copy(spread.at[d, k], terms.at[me], a_own).start()
+
+    z_local.wait()
+    hand_out(0)
+    for i in range(1, max(heads, g.half)):
+        if i < g.half:
+            g.forward(i)
+        if i < heads:
+            z_copies[i - 1].wait_recv()
+            hand_out(i)
+    pltpu.make_async_copy(spread.at[0, 0], terms.at[me], a_own).wait()
+    for j in range(1, n):
+        other = lax.rem(me + j, n)
+        pltpu.make_async_remote_copy(
+            src_ref=terms.at[other], dst_ref=terms.at[other], send_sem=a_send.at[other],
+            recv_sem=a_recv.at[other], device_id={"ctx": other}, device_id_type=MESH,
+        ).wait()
+    g.finish()
+    for c in z_copies:
+        c.wait_send()
+
+    count = out_ref.shape[0]
+    out_ref[...] = jnp.dot(terms[0], att[0], preferred_element_type=jnp.float32)[:count]
+
+    @pl.loop(1, n)
+    def _(s):
+        out_ref[...] += jnp.dot(terms[s], att[s], preferred_element_type=jnp.float32)[:count]
+
+
+def grad_product(low, parts, n, heads, count):
+    rows, width = low.shape
+    halves, padded, _ = parts.shape
+    dma = pltpu.SemaphoreType.DMA
+    return pl.pallas_call(
+        grad_kernel,
+        out_shape=jax.ShapeDtypeStruct((count, width), jnp.float32),
+        in_specs=[pl.BlockSpec(memory_space=pl.ANY)] * 2,
+        out_specs=pl.BlockSpec(memory_space=pltpu.VMEM),
+        scratch_shapes=[
+            pltpu.VMEM((n, rows, width), low.dtype),
+            pltpu.VMEM((heads, halves, padded, rows), parts.dtype),
+            pltpu.VMEM((n, padded, rows), parts.dtype),
+            dma((n - 1,)), dma((n,)), dma,
+            dma((heads,)), dma((heads,)), dma,
+            dma((n,)), dma((n,)), dma,
+        ],
+        compiler_params=pltpu.CompilerParams(
+            collective_id=1, has_side_effects=True, vmem_limit_bytes=32 << 20,
+        ),
+    )(low, parts)
 
 
 def attend_kernel(pairs, lo_ref, hi_ref, slot_ref, q_ref, kv_ref, start_ref, pos_ref,
@@ -116,7 +281,8 @@
     per_kv = heads_local // kv_local
     kv_start = lax.axis_index("head") * heads_local // group
     own_kv = lax.dynamic_slice_in_dim(keys_values, kv_start * 2 * DH, kv_local * 2 * DH, 1)
-    kv = lax.all_gather(own_kv, "ctx", axis=0, tiled=True)
+    n, heads = lax.axis_size("ctx"), lax.axis_size("head")
+    kv = gather(own_kv, n).reshape(n * tokens_local, -1)
 
     tile_count = tile_list.shape[0]
     tiles_local = tokens_local // TILE
@@ -131,12 +297,10 @@
     attended, low = attend(
         queries, kv, lo, hi, slot, start.reshape(-1, 1), pos.reshape(-1, 1), kv_local, per_kv
     )
-    grads = lax.all_gather(grad_rows, "head", axis=1, tiled=True)
-    grads = lax.all_to_all(grads, "ctx", split_axis=1, concat_axis=0, tiled=True)
-    low_all = lax.all_gather(low, "ctx", axis=0, tiled=True)
-    weight_grad = lax.dot_general(
-        grads, low_all, (((0,), (0,)), ((), ())), preferred_element_type=jnp.float32
-    )
+    count = grad_rows.shape[1] * heads // n
+    parts = grad_rows.T.reshape(n // heads, count, tokens_local)
+    parts = jnp.pad(parts, ((0, 0), (0, -count % 16), (0, 0)))
+    weight_grad = grad_product(low, parts, n, heads, count)
     return (attended, weight_grad)
 
 

time: 133 us -> 91.9 us (0.69)
  the two profiles are of different devices: /device:TPU:0 before, /device:TPU:25 now
where the time goes in v2:
time: 91.9 us; the launch traced here: 90.9 us
  Pallas kernels  81.7 us (89%)
  local copies, waits for them, and re-layouts  5.69 us (6%)
  other arithmetic  2.72 us (3%)
    pallas_call x1, Pallas kernels, grad_product(): pl.pallas_call(grad_kernel, out_shape=jax.ShapeDtypeStruct((count, width)...  58.5 us
    pallas_call x1, Pallas kernels, gather(): pl.pallas_call(gather_kernel, out_shape=jax.ShapeDtypeStruct((n,) + x.sha...  12.2 us
    pallas_call x1, Pallas kernels, attend(): pl.pallas_call(functools.partial(attend_kernel, pairs), grid_spec=pltpu.P...  11.1 us
    unnamed x7, local copies, waits for them, and re-layouts  2.34 us

profile of v2, /device:TPU:25, one launch (start us, length us, event | category | flops | bytes accessed | tf_op | source)
XLA Modules:
  0.0 90.9 jit_solution(7867777480985318668)
XLA Ops:
  0.6 0.0 copy-start
  0.6 0.0 copy-start.2
  0.7 0.9 select_reduce_fusion.slot_ref
  1.5 0.7 broadcast_multiply_fusion
  2.3 0.1 iota_add_fusion
  2.3 1.3 %gather_fusion = s32[2,128]{1,0:T(2,128)S(1)} fusion(s32[16,128]{1,0:T(8,128)} %bitcast.9, s32[1024]{0:T(1024)S(1)} %pad_clamp_fusion), kind=kCustom, calls=%fused_computation | custom fusion | bytes 2056 | tf_op jit(solution)/shard_map/gather | solution.py:292
  3.6 1.0 %convert_reduce_fusion = s32[2,128]{1,0:T(2,128)S(1)} fusion(s32[2,128]{1,0:T(2,128)S(1)} %gather_fusion, s32[2048]{0:T(1024)} %param.8), kind=kLoop, calls=%fused_computation.1 | loop fusion | flops 1572608 | bytes 10240 | tf_op jit(solution)/shard_map/reduce_sum | solution.py:293
  4.6 0.1 slice_reduce_fusion
  4.8 0.1 copy.13.pos_ref
  4.9 0.0 copy-done
  4.9 0.7 constant_dynamic-slice_fusion.src_ref
  5.6 0.1 copy.12.start_ref
  5.8 1.0 %pad.4.g_ref = bf16[2,368,256]{2,1,0:T(8,128)(2,1)S(1)} pad(bf16[2,360,256]{2,1,0:T(8,128)(2,1)} %bitcast.8, bf16[]{:T(256)} %constant.51.clone.1), padding=0_0x0_8x0_0 | pad | bytes 745474 | tf_op jit(solution)/shard_map/jit(_pad)/pad | solution.py:302
  6.8 12.2 %shard_map.68 = bf16[8,256,256]{2,1,0:T(8,128)(2,1)} custom-call(bf16[256,256]{1,0:T(8,128)(2,1)} %constant_dynamic-slice_fusion.src_ref), custom_call_target="tpu_custom_call" | custom-call | tf_op jit(solution)/shard_map/pallas_call | solution.py:82
  18.9 0.0 copy-done.2
  19.0 0.0 copy-start.1
  19.0 1.2 %copy-done.1 = bf16[8,256,256]{2,1,0:T(8,128)(2,1)S(1)} copy-done((bf16[8,256,256]{2,1,0:T(8,128)(2,1)S(1)}, bf16[8,256,256]{2,1,0:T(8,128)(2,1)}, u32[]{:S(2)}) %copy-start.1) | copy-done | bytes 1048600
  20.2 11.1 %shard_map.69 = (f32[256,1024]{1,0:T(8,128)}, bf16[256,1024]{1,0:T(8,128)(2,1)S(1)}) custom-call(s32[2]{0:T(128)S(1)} %and_select_fusion.lo_ref, s32[2]{0:T(128)S(1)} %get-tuple-element.7.hi_ref, s32[16]{0:T(128)S(1)} %select_reduce_fusion.slot_ref, bf16[256,1024]{1,0:T(8,128)(2,1)S(1)} %copy-done.2, bf16[2048,256]{1,0:T(8,128)(2,1)S(1)} %bitcast.7, ...), custom_call_target="tpu_custom_call" | custom-call | flops 536870912 | bytes 3145728 | tf_op jit(solution)/shard_map/pallas_call | solution.py:250
  31.3 58.5 %shard_map.70 = f32[360,1024]{1,0:T(8,128)S(1)} custom-call(bf16[256,1024]{1,0:T(8,128)(2,1)S(1)} %get-tuple-element.5.low_ref, bf16[2,368,256]{2,1,0:T(8,128)(2,1)S(1)} %pad.4.g_ref), custom_call_target="tpu_custom_call" | custom-call | tf_op jit(solution)/shard_map/pallas_call | solution.py:163
  89.7 1.1 %copy.15 = f32[360,1024]{1,0:T(8,128)} copy(f32[360,1024]{1,0:T(8,128)S(1)} %shard_map.70) | data formatting | bytes 2949120
  (3 shorter events, 0.0 us)
Async XLA Ops:
  0.6 4.3 %copy-start = (bf16[256,1024]{1,0:T(8,128)(2,1)S(1)}, bf16[256,1024]{1,0:T(8,128)(2,1)}, u32[]{:S(2)}) copy-start(bf16[256,1024]{1,0:T(8,128)(2,1)} %param.6) | copy-start | bytes 1572868
  0.6 18.3 %copy-start.2 = (bf16[256,1024]{1,0:T(8,128)(2,1)S(1)}, bf16[256,1024]{1,0:T(8,128)(2,1)}, u32[]{:S(2)}) copy-start(bf16[256,1024]{1,0:T(8,128)(2,1)} %q_ref.1) | copy-start | bytes 1572868
  19.0 1.2 %copy-start.1 = (bf16[8,256,256]{2,1,0:T(8,128)(2,1)S(1)}, bf16[8,256,256]{2,1,0:T(8,128)(2,1)}, u32[]{:S(2)}) copy-start(bf16[8,256,256]{2,1,0:T(8,128)(2,1)} %shard_map.68) | copy-start | bytes 3145732

commit v3 on v2

--- a/solution.py
+++ b/solution.py
@@ -68,85 +68,201 @@
             c.wait_send()
 
 
-def gather_kernel(src_ref, slots_ref, send, recv, own):
-    n = slots_ref.shape[0]
-    greet(n, 0)
-    g = Gather(src_ref, slots_ref, send, recv, own)
+class Spread:
+    def __init__(self, parts_of, slots, terms, right, left, recv, a_send, a_recv, a_own):
+        self.heads, self.halves, self.n = slots.shape[0], slots.shape[1], terms.shape[0]
+        self.parts_of, self.slots, self.terms = parts_of, slots, terms
+        self.right, self.left, self.recv = right, left, recv
+        self.a_send, self.a_recv, self.a_own = a_send, a_recv, a_own
+        self.me, self.head = lax.axis_index("ctx"), lax.axis_index("head")
+
+    def hop_copy(self, i, owner, to, send):
+        return pltpu.make_async_remote_copy(
+            src_ref=self.parts_of(i - 1, owner), dst_ref=self.slots.at[owner], send_sem=send.at[i],
+            recv_sem=self.recv.at[owner], device_id={"head": to}, device_id_type=MESH,
+        )
+
+    def each_sent(self, i, act):
+        head, heads = self.head, self.heads
+        to_right, to_left = head - (i - 1), head + (i - 1)
+
+        @pl.when((to_right >= 0) & (head + 1 < heads))
+        def _():
+            act(self.hop_copy(i, to_right, head + 1, self.right))
+
+        @pl.when((to_left < heads) & (head >= 1))
+        def _():
+            act(self.hop_copy(i, to_left, head - 1, self.left))
+
+    def start_hop(self, i):
+        self.each_sent(i, lambda c: c.start())
+
+    def end_hop(self, i):
+        self.each_sent(i, lambda c: c.wait_send())
+
+    def each_owner(self, i, act):
+        if i == 0:
+            act(self.head)
+            return
+
+        @pl.when(self.head >= i)
+        def _():
+            act(self.head - i)
+
+        @pl.when(self.head + i < self.heads)
+        def _():
+            act(self.head + i)
+
+    def arrive(self, i):
+        def wait(owner):
+            pltpu.make_async_remote_copy(
+                src_ref=self.slots.at[owner], dst_ref=self.slots.at[owner], send_sem=self.right.at[i],
+                recv_sem=self.recv.at[owner], device_id={"head": owner}, device_id_type=MESH,
+            ).wait_recv()
+
+        self.each_owner(i, wait)
+
+    def each_block(self, i, remote, local):
+        def blocks(owner):
+            for k in range(self.halves):
+                to = owner * self.halves + k
+                src = self.parts_of(i, owner).at[k]
+
+                @pl.when(to != self.me)
+                def _():
+                    remote(pltpu.make_async_remote_copy(
+                        src_ref=src, dst_ref=self.terms.at[self.me], send_sem=self.a_send.at[to],
+                        recv_sem=self.a_recv.at[self.me], device_id={"ctx": to}, device_id_type=MESH,
+                    ))
+
+                @pl.when(to == self.me)
+                def _():
+                    local(pltpu.make_async_copy(src, self.terms.at[self.me], self.a_own))
+
+        self.each_owner(i, blocks)
+
+    def hand_out(self, i):
+        self.each_block(i, lambda c: c.start(), lambda c: c.start())
+
+    def end_hand_out(self, i):
+        self.each_block(i, lambda c: c.wait_send(), lambda c: c.wait())
+
+    def wait_terms(self):
+        for j in range(1, self.n):
+            other = lax.rem(self.me + j, self.n)
+            pltpu.make_async_remote_copy(
+                src_ref=self.terms.at[other], dst_ref=self.terms.at[other], send_sem=self.a_send.at[other],
+                recv_sem=self.a_recv.at[other], device_id={"ctx": other}, device_id_type=MESH,
+            ).wait_recv()
+
+
+def is_near(halves):
+    gap = lax.axis_index("head") - lax.axis_index("ctx") // halves
+    return (gap <= 1) & (gap >= -1)
+
+
+def first_kernel(kv_ref, g_ref, all_ref, slots_ref, terms_ref, send, recv, own,
+                 right, left, z_recv, a_send, a_recv, a_own):
+    n, heads, halves = all_ref.shape[0], slots_ref.shape[0], slots_ref.shape[1]
+    greet(n, heads)
+    sp = Spread(
+        lambda i, owner: g_ref if i == 0 else slots_ref.at[owner],
+        slots_ref, terms_ref, right, left, z_recv, a_send, a_recv, a_own,
+    )
+    g = Gather(kv_ref, all_ref, send, recv, own)
+    hops = min(2, heads - 1)
     g.start()
+    sp.start_hop(1)
+    sp.hand_out(0)
     for j in range(1, g.half):
         g.forward(j)
+    for i in range(1, hops + 1):
+        sp.arrive(i)
+        if i < hops:
+            sp.start_hop(i + 1)
+        if i == 1:
+            sp.hand_out(1)
+
+    @pl.when(is_near(halves))
+    def _():
+        sp.wait_terms()
+
+    for i in (0, 1):
+        sp.end_hand_out(i)
+    for i in range(1, hops + 1):
+        sp.end_hop(i)
     g.finish()
 
 
-def gather(x, n):
+def spread_sems(n, heads):
+    dma = pltpu.SemaphoreType.DMA
+    return [
+        dma((n - 1,)), dma((n,)), dma,
+        dma((heads,)), dma((heads,)), dma((heads,)),
+        dma((n,)), dma((n,)), dma,
+    ]
+
+
+def first_moves(kv, parts, n, heads):
+    whole = pl.BlockSpec(memory_space=pl.ANY)
+    halves, padded, rows = parts.shape
     return pl.pallas_call(
-        gather_kernel,
-        out_shape=jax.ShapeDtypeStruct((n,) + x.shape, x.dtype),
-        in_specs=[pl.BlockSpec(memory_space=pl.ANY)],
-        out_specs=pl.BlockSpec(memory_space=pl.ANY),
-        scratch_shapes=[
-            pltpu.SemaphoreType.DMA((n - 1,)), pltpu.SemaphoreType.DMA((n,)), pltpu.SemaphoreType.DMA,
+        first_kernel,
+        out_shape=[
+            jax.ShapeDtypeStruct((n,) + kv.shape, kv.dtype),
+            jax.ShapeDtypeStruct((heads,) + parts.shape, parts.dtype),
+            jax.ShapeDtypeStruct((n, padded, rows), parts.dtype),
         ],
+        in_specs=[whole] * 2,
+        out_specs=[whole] * 3,
+        scratch_shapes=spread_sems(n, heads),
         compiler_params=pltpu.CompilerParams(collective_id=0, has_side_effects=True),
-    )(x)
-
-
-def grad_kernel(low_ref, g_ref, out_ref, att, spread, terms, send, recv, own,
-                z_send, z_recv, z_own, a_send, a_recv, a_own):
-    n, heads, halves = att.shape[0], spread.shape[0], spread.shape[1]
-    me, head = lax.axis_index("ctx"), lax.axis_index("head")
+    )(kv, parts)
+
+
+def grad_kernel(low_ref, early_ref, near_ref, out_ref, att, slots, terms, copied, send, recv, own,
+                right, left, z_recv, a_send, a_recv, a_own):
+    n, heads, halves = att.shape[0], slots.shape[0], slots.shape[1]
     greet(n, heads)
-
-    z_copies = [
-        pltpu.make_async_remote_copy(
-            src_ref=g_ref, dst_ref=spread.at[d], send_sem=z_send.at[d], recv_sem=z_recv.at[d],
-            device_id={"head": lax.rem(head + d, heads)}, device_id_type=MESH,
-        )
-        for d in range(1, heads)
-    ]
-    for c in z_copies:
-        c.start()
-    z_local = pltpu.make_async_copy(g_ref, spread.at[0], z_own)
-    z_local.start()
+    sp = Spread(
+        lambda i, owner: (early_ref if i <= 2 else slots).at[owner],
+        slots, terms, right, left, z_recv, a_send, a_recv, a_own,
+    )
     g = Gather(low_ref, att, send, recv, own)
+    near = is_near(halves)
+    if heads > 3:
+        sp.start_hop(3)
+    if heads > 2:
+        sp.hand_out(2)
     g.start()
 
-    def block(src, to):
-        return pltpu.make_async_remote_copy(
-            src_ref=src, dst_ref=terms.at[me], send_sem=a_send.at[to], recv_sem=a_recv.at[me],
-            device_id={"ctx": to}, device_id_type=MESH,
-        )
-
-    def hand_out(d):
-        for k in range(halves):
-            to = lax.rem(head + heads - d, heads) * halves + k
-
-            @pl.when(to != me)
-            def _():
-                block(spread.at[d, k], to).start()
-
-            @pl.when(to == me)
-            def _():
-                pltpu.make_async_copy(spread.at[d, k], terms.at[me], a_own).start()
-
-    z_local.wait()
-    hand_out(0)
-    for i in range(1, max(heads, g.half)):
+    @pl.when(near)
+    def _():
+        pltpu.make_async_copy(near_ref, terms, copied).start()
+
+    for i in range(1, max(heads - 2, g.half)):
         if i < g.half:
             g.forward(i)
-        if i < heads:
-            z_copies[i - 1].wait_recv()
-            hand_out(i)
-    pltpu.make_async_copy(spread.at[0, 0], terms.at[me], a_own).wait()
-    for j in range(1, n):
-        other = lax.rem(me + j, n)
-        pltpu.make_async_remote_copy(
-            src_ref=terms.at[other], dst_ref=terms.at[other], send_sem=a_send.at[other],
-            recv_sem=a_recv.at[other], device_id={"ctx": other}, device_id_type=MESH,
-        ).wait()
+        if i + 2 < heads:
+            sp.arrive(i + 2)
+            if i + 3 < heads:
+                sp.start_hop(i + 3)
+            sp.hand_out(i + 2)
+
+    @pl.when(near)
+    def _():
+        pltpu.make_async_copy(near_ref, terms, copied).wait()
+
+    for i in range(2, heads):
+        sp.end_hand_out(i)
+
+    @pl.when(jnp.logical_not(near))
+    def _():
+        sp.wait_terms()
+
+    for i in range(3, heads):
+        sp.end_hop(i)
     g.finish()
-    for c in z_copies:
-        c.wait_send()
 
     count = out_ref.shape[0]
     out_ref[...] = jnp.dot(terms[0], att[0], preferred_element_type=jnp.float32)[:count]
@@ -156,27 +272,25 @@
         out_ref[...] += jnp.dot(terms[s], att[s], preferred_element_type=jnp.float32)[:count]
 
 
-def grad_product(low, parts, n, heads, count):
+def grad_product(low, early, near, count):
     rows, width = low.shape
-    halves, padded, _ = parts.shape
-    dma = pltpu.SemaphoreType.DMA
+    heads, n = early.shape[0], near.shape[0]
+    whole = pl.BlockSpec(memory_space=pl.ANY)
     return pl.pallas_call(
         grad_kernel,
         out_shape=jax.ShapeDtypeStruct((count, width), jnp.float32),
-        in_specs=[pl.BlockSpec(memory_space=pl.ANY)] * 2,
+        in_specs=[whole] * 3,
         out_specs=pl.BlockSpec(memory_space=pltpu.VMEM),
         scratch_shapes=[
             pltpu.VMEM((n, rows, width), low.dtype),
-            pltpu.VMEM((heads, halves, padded, rows), parts.dtype),
-            pltpu.VMEM((n, padded, rows), parts.dtype),
-            dma((n - 1,)), dma((n,)), dma,
-            dma((heads,)), dma((heads,)), dma,
-            dma((n,)), dma((n,)), dma,
-        ],
+            pltpu.VMEM(early.shape, early.dtype),
+            pltpu.VMEM(near.shape, near.dtype),
+            pltpu.SemaphoreType.DMA,
+        ] + spread_sems(n, heads),
         compiler_params=pltpu.CompilerParams(
             collective_id=1, has_side_effects=True, vmem_limit_bytes=32 << 20,
         ),
-    )(low, parts)
+    )(low, early, near)
 
 
 def attend_kernel(pairs, lo_ref, hi_ref, slot_ref, q_ref, kv_ref, start_ref, pos_ref,
@@ -282,7 +396,11 @@
     kv_start = lax.axis_index("head") * heads_local // group
     own_kv = lax.dynamic_slice_in_dim(keys_values, kv_start * 2 * DH, kv_local * 2 * DH, 1)
     n, heads = lax.axis_size("ctx"), lax.axis_size("head")
-    kv = gather(own_kv, n).reshape(n * tokens_local, -1)
+    count = grad_rows.shape[1] * heads // n
+    parts = grad_rows.T.reshape(n // heads, count, tokens_local)
+    parts = jnp.pad(parts, ((0, 0), (0, -count % 16), (0, 0)))
+    kv, early, near = first_moves(own_kv, parts, n, heads)
+    kv = kv.reshape(n * tokens_local, -1)
 
     tile_count = tile_list.shape[0]
     tiles_local = tokens_local // TILE
@@ -297,10 +415,7 @@
     attended, low = attend(
         queries, kv, lo, hi, slot, start.reshape(-1, 1), pos.reshape(-1, 1), kv_local, per_kv
     )
-    count = grad_rows.shape[1] * heads // n
-    parts = grad_rows.T.reshape(n // heads, count, tokens_local)
-    parts = jnp.pad(parts, ((0, 0), (0, -count % 16), (0, 0)))
-    weight_grad = grad_product(low, parts, n, heads, count)
+    weight_grad = grad_product(low, early, near, count)
     return (attended, weight_grad)
 
 

time: 91.9 us -> 101 us (1.099)
  the two profiles are of different devices: /device:TPU:25 before, /device:TPU:17 now
where the time goes in v3:
time: 101 us; the launch traced here: 102 us
  Pallas kernels  91.7 us (91%)
  local copies, waits for them, and re-layouts  6.43 us (6%)
  other arithmetic  2.73 us (3%)
    pallas_call x1, Pallas kernels, grad_product(): pl.pallas_call(grad_kernel, out_shape=jax.ShapeDtypeStruct((count, width)...  52.2 us
    pallas_call x1, Pallas kernels, first_moves(): pl.pallas_call(first_kernel, out_shape=[jax.ShapeDtypeStruct((n,) + kv.sh...  29.6 us
    pallas_call x1, Pallas kernels, attend(): pl.pallas_call(functools.partial(attend_kernel, pairs), grid_spec=pltpu.P...  9.87 us
    unnamed x11, local copies, waits for them, and re-layouts  2.35 us

profile of v3, /device:TPU:17, one launch (start us, length us, event | category | flops | bytes accessed | tf_op | source)
XLA Modules:
  0.0 101.5 jit_solution(10144936620345687483)
XLA Ops:
  0.6 0.0 copy-start
  0.6 0.0 copy-start.4
  0.7 0.8 broadcast_multiply_fusion
  1.5 1.3 %gather_fusion = s32[2,128]{1,0:T(2,128)S(1)} fusion(s32[16,128]{1,0:T(8,128)} %bitcast.9, s32[1024]{0:T(1024)S(1)} %pad_clamp_fusion), kind=kCustom, calls=%fused_computation | custom fusion | bytes 2056 | tf_op jit(solution)/shard_map/gather | solution.py:410
  2.7 1.0 %convert_reduce_fusion = s32[2,128]{1,0:T(2,128)S(1)} fusion(s32[2,128]{1,0:T(2,128)S(1)} %gather_fusion, s32[2048]{0:T(1024)} %param.8), kind=kLoop, calls=%fused_computation.1 | loop fusion | flops 1572608 | bytes 10240 | tf_op jit(solution)/shard_map/reduce_sum | solution.py:411
  3.8 0.1 slice_reduce_fusion
  3.9 0.8 select_reduce_fusion.slot_ref
  4.7 0.0 copy-done
  4.7 0.7 constant_dynamic-slice_fusion.kv_ref
  5.4 1.8 %pad.4.g_ref = bf16[2,368,256]{2,1,0:T(8,128)(2,1)} pad(bf16[2,360,256]{2,1,0:T(8,128)(2,1)} %bitcast.8, bf16[]{:T(256)} %constant.51.clone.1), padding=0_0x0_8x0_0 | pad | bytes 745474 | tf_op jit(solution)/shard_map/jit(_pad)/pad | solution.py:401
  7.2 29.6 %shard_map.68 = (bf16[8,256,256]{2,1,0:T(8,128)(2,1)}, bf16[4,2,368,256]{3,2,1,0:T(8,128)(2,1)}, bf16[8,368,256]{2,1,0:T(8,128)(2,1)}) custom-call(bf16[256,256]{1,0:T(8,128)(2,1)} %constant_dynamic-slice_fusion.kv_ref, bf16[2,368,256]{2,1,0:T(8,128)(2,1)} %pad.4.g_ref), custom_call_target="tpu_custom_call" | custom-call | tf_op jit(solution)/shard_map/pallas_call | solution.py:209
  36.8 0.1 copy.12.start_ref
  36.9 0.1 iota_add_fusion
  37.0 0.1 copy.13.pos_ref
  37.1 0.0 copy-done.4
  37.1 0.0 copy-start.3
  37.1 1.2 %copy-done.3 = bf16[8,256,256]{2,1,0:T(8,128)(2,1)S(1)} copy-done((bf16[8,256,256]{2,1,0:T(8,128)(2,1)S(1)}, bf16[8,256,256]{2,1,0:T(8,128)(2,1)}, u32[]{:S(2)}) %copy-start.3) | copy-done | bytes 1048600
  38.4 0.0 copy-start.1
  38.4 0.0 copy-start.2
  38.4 9.9 %shard_map.69 = (f32[256,1024]{1,0:T(8,128)}, bf16[256,1024]{1,0:T(8,128)(2,1)S(1)}) custom-call(s32[2]{0:T(128)S(1)} %and_select_fusion.lo_ref, s32[2]{0:T(128)S(1)} %get-tuple-element.13.hi_ref, s32[16]{0:T(128)S(1)} %select_reduce_fusion.slot_ref, bf16[256,1024]{1,0:T(8,128)(2,1)S(1)} %copy-done.4, bf16[2048,256]{1,0:T(8,128)(2,1)S(1)} %bitcast.7, ...), custom_call_target="tpu_custom_call" | custom-call | flops 536870912 | bytes 3145728 | tf_op jit(solution)/shard_map/pallas_call | solution.py:364
  48.2 0.0 copy-done.1
  48.2 0.0 copy-done.2
  48.2 52.2 %shard_map.70 = f32[360,1024]{1,0:T(8,128)S(1)} custom-call(bf16[256,1024]{1,0:T(8,128)(2,1)S(1)} %get-tuple-element.9.low_ref, bf16[4,2,368,256]{3,2,1,0:T(8,128)(2,1)S(1)} %copy-done.1, bf16[8,368,256]{2,1,0:T(8,128)(2,1)S(1)} %copy-done.2), custom_call_target="tpu_custom_call" | custom-call | tf_op jit(solution)/shard_map/pallas_call | solution.py:279
  100.4 1.1 %copy.15 = f32[360,1024]{1,0:T(8,128)} copy(f32[360,1024]{1,0:T(8,128)S(1)} %shard_map.70) | data formatting | bytes 2949120
  (3 shorter events, 0.0 us)
Async XLA Ops:
  0.6 4.1 %copy-start = (bf16[256,1024]{1,0:T(8,128)(2,1)S(1)}, bf16[256,1024]{1,0:T(8,128)(2,1)}, u32[]{:S(2)}) copy-start(bf16[256,1024]{1,0:T(8,128)(2,1)} %param.6) | copy-start | bytes 1572868
  0.6 36.5 %copy-start.4 = (bf16[256,1024]{1,0:T(8,128)(2,1)S(1)}, bf16[256,1024]{1,0:T(8,128)(2,1)}, u32[]{:S(2)}) copy-start(bf16[256,1024]{1,0:T(8,128)(2,1)} %q_ref.1) | copy-start | bytes 1572868
  37.1 1.2 %copy-start.3 = (bf16[8,256,256]{2,1,0:T(8,128)(2,1)S(1)}, bf16[8,256,256]{2,1,0:T(8,128)(2,1)}, u32[]{:S(2)}) copy-start(bf16[8,256,256]{2,1,0:T(8,128)(2,1)} %get-tuple-element.7) | copy-start | bytes 3145732
  38.4 9.9 %copy-start.1 = (bf16[4,2,368,256]{3,2,1,0:T(8,128)(2,1)S(1)}, bf16[4,2,368,256]{3,2,1,0:T(8,128)(2,1)}, u32[]{:S(2)}) copy-start(bf16[4,2,368,256]{3,2,1,0:T(8,128)(2,1)} %get-tuple-element.10.early_ref) | copy-start | bytes 4521988
  38.4 9.9 %copy-start.2 = (bf16[8,368,256]{2,1,0:T(8,128)(2,1)S(1)}, bf16[8,368,256]{2,1,0:T(8,128)(2,1)}, u32[]{:S(2)}) copy-start(bf16[8,368,256]{2,1,0:T(8,128)(2,1)} %get-tuple-element.11.near_ref) | copy-start | bytes 4521988

commit v4 on v3

--- a/solution.py
+++ b/solution.py
@@ -36,9 +36,15 @@
         self.mate = self.pair * 2 + 1 - self.side
         self.slots, self.send, self.recv = slots, send, recv
         self.local = pltpu.make_async_copy(src, slots.at[me], own)
-        self.sends = [
-            self.copy(src, me, lax.rem(self.pair + j, half) * 2 + self.side, j - 1) for j in range(1, half)
-        ]
+        if half == 4:
+            pair = self.pair
+            self.near = (pair + 1 - 2 * (pair % 2)) * 2 + self.side
+            self.next = lax.rem(pair + 2, 4) * 2 + self.side
+            self.far = (3 - pair) * 2 + self.side
+            targets = [self.near, self.next]
+        else:
+            targets = [lax.rem(self.pair + j, half) * 2 + self.side for j in range(1, half)]
+        self.sends = [self.copy(src, me, to, i) for i, to in enumerate(targets)]
         self.sends.append(self.copy(src, me, self.mate, half - 1))
 
     def copy(self, src, owner, to, i):
@@ -47,12 +53,39 @@
             recv_sem=self.recv.at[owner], device_id={"ctx": to}, device_id_type=MESH,
         )
 
+    def part(self, owner, which, to, i):
+        rows = self.slots.shape[1] // 2
+        ref = self.slots.at[owner, pl.ds(which * rows, rows)]
+        return pltpu.make_async_remote_copy(
+            src_ref=ref, dst_ref=ref, send_sem=self.send.at[i],
+            recv_sem=self.recv.at[owner + which * self.n], device_id={"ctx": to}, device_id_type=MESH,
+        )
+
     def start(self):
         for c in self.sends:
             c.start()
         self.local.start()
 
+    def square(self, j):
+        if j < 3:
+            owner, to = (self.near, self.next) if j == 1 else (self.next, self.near)
+            c = self.copy(self.slots.at[owner], owner, self.mate, 3 + j)
+            c.wait_recv()
+            half = self.part(owner, j - 1, to, 6 + j)
+            half.start()
+            self.sends.append(half)
+        else:
+            owner = self.far
+            for which in range(2):
+                self.part(owner, which, self.mate, 0).wait_recv()
+            c = self.copy(self.slots.at[owner], owner, self.mate, 3 + j)
+        c.start()
+        self.sends.append(c)
+
     def forward(self, j):
+        if self.half == 4:
+            self.square(j)
+            return
         owner = lax.rem(self.pair + self.half - j, self.half) * 2 + self.side
         c = self.copy(self.slots.at[owner], owner, self.mate, self.half - 1 + j)
         c.wait_recv()
@@ -158,7 +191,7 @@
 
 def is_near(halves):
     gap = lax.axis_index("head") - lax.axis_index("ctx") // halves
-    return (gap <= 1) & (gap >= -1)
+    return gap == 0
 
 
 def first_kernel(kv_ref, g_ref, all_ref, slots_ref, terms_ref, send, recv, own,
@@ -170,34 +203,26 @@
         slots_ref, terms_ref, right, left, z_recv, a_send, a_recv, a_own,
     )
     g = Gather(kv_ref, all_ref, send, recv, own)
-    hops = min(2, heads - 1)
     g.start()
     sp.start_hop(1)
     sp.hand_out(0)
     for j in range(1, g.half):
         g.forward(j)
-    for i in range(1, hops + 1):
-        sp.arrive(i)
-        if i < hops:
-            sp.start_hop(i + 1)
-        if i == 1:
-            sp.hand_out(1)
+    sp.arrive(1)
 
     @pl.when(is_near(halves))
     def _():
         sp.wait_terms()
 
-    for i in (0, 1):
-        sp.end_hand_out(i)
-    for i in range(1, hops + 1):
-        sp.end_hop(i)
+    sp.end_hand_out(0)
+    sp.end_hop(1)
     g.finish()
 
 
 def spread_sems(n, heads):
     dma = pltpu.SemaphoreType.DMA
     return [
-        dma((n - 1,)), dma((n,)), dma,
+        dma((2 * n,)), dma((2 * n,)), dma,
         dma((heads,)), dma((heads,)), dma((heads,)),
         dma((n,)), dma((n,)), dma,
     ]
@@ -225,42 +250,40 @@
     n, heads, halves = att.shape[0], slots.shape[0], slots.shape[1]
     greet(n, heads)
     sp = Spread(
-        lambda i, owner: (early_ref if i <= 2 else slots).at[owner],
+        lambda i, owner: (early_ref if i <= 1 else slots).at[owner],
         slots, terms, right, left, z_recv, a_send, a_recv, a_own,
     )
     g = Gather(low_ref, att, send, recv, own)
     near = is_near(halves)
-    if heads > 3:
-        sp.start_hop(3)
-    if heads > 2:
-        sp.hand_out(2)
     g.start()
+    sp.start_hop(2)
+    sp.hand_out(1)
 
     @pl.when(near)
     def _():
         pltpu.make_async_copy(near_ref, terms, copied).start()
 
-    for i in range(1, max(heads - 2, g.half)):
+    for i in range(1, max(heads - 1, g.half)):
+        if i + 1 < heads:
+            sp.arrive(i + 1)
+            if i + 2 < heads:
+                sp.start_hop(i + 2)
+            sp.hand_out(i + 1)
         if i < g.half:
             g.forward(i)
-        if i + 2 < heads:
-            sp.arrive(i + 2)
-            if i + 3 < heads:
-                sp.start_hop(i + 3)
-            sp.hand_out(i + 2)
 
     @pl.when(near)
     def _():
         pltpu.make_async_copy(near_ref, terms, copied).wait()
 
-    for i in range(2, heads):
+    for i in range(1, heads):
         sp.end_hand_out(i)
 
     @pl.when(jnp.logical_not(near))
     def _():
         sp.wait_terms()
 
-    for i in range(3, heads):
+    for i in range(2, heads):
         sp.end_hop(i)
     g.finish()
 

time: 101 us -> 92.8 us (0.919)
  the two profiles are of different devices: /device:TPU:17 before, /device:TPU:3 now
where the time goes in v4:
time: 92.8 us; the launch traced here: 93.1 us
  Pallas kernels  83.3 us (90%)
  local copies, waits for them, and re-layouts  6.43 us (7%)
  other arithmetic  2.73 us (3%)
    pallas_call x1, Pallas kernels, grad_product(): pl.pallas_call(grad_kernel, out_shape=jax.ShapeDtypeStruct((count, width)...  52.1 us
    pallas_call x1, Pallas kernels, first_moves(): pl.pallas_call(first_kernel, out_shape=[jax.ShapeDtypeStruct((n,) + kv.sh...  22.5 us
    pallas_call x1, Pallas kernels, attend(): pl.pallas_call(functools.partial(attend_kernel, pairs), grid_spec=pltpu.P...  8.65 us
    unnamed x11, local copies, waits for them, and re-layouts  2.35 us

profile of v4, /device:TPU:3, one launch (start us, length us, event | category | flops | bytes accessed | tf_op | source)
XLA Modules:
  0.0 93.1 jit_solution(7170985251675608286)
XLA Ops:
  0.6 0.0 copy-start
  0.6 0.0 copy-start.4
  0.7 0.8 broadcast_multiply_fusion
  1.5 1.3 %gather_fusion = s32[2,128]{1,0:T(2,128)S(1)} fusion(s32[16,128]{1,0:T(8,128)} %bitcast.9, s32[1024]{0:T(1024)S(1)} %pad_clamp_fusion), kind=kCustom, calls=%fused_computation | custom fusion | bytes 2056 | tf_op jit(solution)/shard_map/gather | solution.py:433
  2.7 1.0 %convert_reduce_fusion = s32[2,128]{1,0:T(2,128)S(1)} fusion(s32[2,128]{1,0:T(2,128)S(1)} %gather_fusion, s32[2048]{0:T(1024)} %param.8), kind=kLoop, calls=%fused_computation.1 | loop fusion | flops 1572608 | bytes 10240 | tf_op jit(solution)/shard_map/reduce_sum | solution.py:434
  3.8 0.1 slice_reduce_fusion
  3.9 0.8 select_reduce_fusion.slot_ref
  4.7 0.0 copy-done
  4.7 0.7 constant_dynamic-slice_fusion.kv_ref
  5.4 1.8 %pad.4.g_ref = bf16[2,368,256]{2,1,0:T(8,128)(2,1)} pad(bf16[2,360,256]{2,1,0:T(8,128)(2,1)} %bitcast.8, bf16[]{:T(256)} %constant.51.clone.1), padding=0_0x0_8x0_0 | pad | bytes 745474 | tf_op jit(solution)/shard_map/jit(_pad)/pad | solution.py:424
  7.2 22.5 %shard_map.68 = (bf16[8,256,256]{2,1,0:T(8,128)(2,1)}, bf16[4,2,368,256]{3,2,1,0:T(8,128)(2,1)}, bf16[8,368,256]{2,1,0:T(8,128)(2,1)}) custom-call(bf16[256,256]{1,0:T(8,128)(2,1)} %constant_dynamic-slice_fusion.kv_ref, bf16[2,368,256]{2,1,0:T(8,128)(2,1)} %pad.4.g_ref), custom_call_target="tpu_custom_call" | custom-call | tf_op jit(solution)/shard_map/pallas_call | solution.py:234
  29.6 0.1 copy.12.start_ref
  29.8 0.1 iota_add_fusion
  29.9 0.1 copy.13.pos_ref
  30.0 0.0 copy-done.4
  30.0 0.0 copy-start.3
  30.0 1.2 %copy-done.3 = bf16[8,256,256]{2,1,0:T(8,128)(2,1)S(1)} copy-done((bf16[8,256,256]{2,1,0:T(8,128)(2,1)S(1)}, bf16[8,256,256]{2,1,0:T(8,128)(2,1)}, u32[]{:S(2)}) %copy-start.3) | copy-done | bytes 1048600
  31.2 0.0 copy-start.1
  31.2 0.0 copy-start.2
  31.2 8.7 %shard_map.69 = (f32[256,1024]{1,0:T(8,128)}, bf16[256,1024]{1,0:T(8,128)(2,1)S(1)}) custom-call(s32[2]{0:T(128)S(1)} %and_select_fusion.lo_ref, s32[2]{0:T(128)S(1)} %get-tuple-element.13.hi_ref, s32[16]{0:T(128)S(1)} %select_reduce_fusion.slot_ref, bf16[256,1024]{1,0:T(8,128)(2,1)S(1)} %copy-done.4, bf16[2048,256]{1,0:T(8,128)(2,1)S(1)} %bitcast.7, ...), custom_call_target="tpu_custom_call" | custom-call | flops 536870912 | bytes 3145728 | tf_op jit(solution)/shard_map/pallas_call | solution.py:387
  39.9 0.0 copy-done.1
  39.9 0.0 copy-done.2
  39.9 52.1 %shard_map.70 = f32[360,1024]{1,0:T(8,128)S(1)} custom-call(bf16[256,1024]{1,0:T(8,128)(2,1)S(1)} %get-tuple-element.9.low_ref, bf16[4,2,368,256]{3,2,1,0:T(8,128)(2,1)S(1)} %copy-done.1, bf16[8,368,256]{2,1,0:T(8,128)(2,1)S(1)} %copy-done.2), custom_call_target="tpu_custom_call" | custom-call | tf_op jit(solution)/shard_map/pallas_call | solution.py:302
  92.0 1.1 %copy.15 = f32[360,1024]{1,0:T(8,128)} copy(f32[360,1024]{1,0:T(8,128)S(1)} %shard_map.70) | data formatting | bytes 2949120
  (3 shorter events, 0.0 us)
Async XLA Ops:
  0.6 4.1 %copy-start = (bf16[256,1024]{1,0:T(8,128)(2,1)S(1)}, bf16[256,1024]{1,0:T(8,128)(2,1)}, u32[]{:S(2)}) copy-start(bf16[256,1024]{1,0:T(8,128)(2,1)} %param.6) | copy-start | bytes 1572868
  0.6 29.4 %copy-start.4 = (bf16[256,1024]{1,0:T(8,128)(2,1)S(1)}, bf16[256,1024]{1,0:T(8,128)(2,1)}, u32[]{:S(2)}) copy-start(bf16[256,1024]{1,0:T(8,128)(2,1)} %q_ref.1) | copy-start | bytes 1572868
  30.0 1.2 %copy-start.3 = (bf16[8,256,256]{2,1,0:T(8,128)(2,1)S(1)}, bf16[8,256,256]{2,1,0:T(8,128)(2,1)}, u32[]{:S(2)}) copy-start(bf16[8,256,256]{2,1,0:T(8,128)(2,1)} %get-tuple-element.7) | copy-start | bytes 3145732
  31.2 8.7 %copy-start.1 = (bf16[4,2,368,256]{3,2,1,0:T(8,128)(2,1)S(1)}, bf16[4,2,368,256]{3,2,1,0:T(8,128)(2,1)}, u32[]{:S(2)}) copy-start(bf16[4,2,368,256]{3,2,1,0:T(8,128)(2,1)} %get-tuple-element.10.early_ref) | copy-start | bytes 4521988
  31.2 8.7 %copy-start.2 = (bf16[8,368,256]{2,1,0:T(8,128)(2,1)S(1)}, bf16[8,368,256]{2,1,0:T(8,128)(2,1)}, u32[]{:S(2)}) copy-start(bf16[8,368,256]{2,1,0:T(8,128)(2,1)} %get-tuple-element.11.near_ref) | copy-start | bytes 4521988

commit v5 on v4

--- a/solution.py
+++ b/solution.py
@@ -103,7 +103,7 @@
 
 class Spread:
     def __init__(self, parts_of, slots, terms, right, left, recv, a_send, a_recv, a_own):
-        self.heads, self.halves, self.n = slots.shape[0], slots.shape[1], terms.shape[0]
+        self.heads, self.halves, self.n = slots.shape[0], slots.shape[1], lax.axis_size("ctx")
         self.parts_of, self.slots, self.terms = parts_of, slots, terms
         self.right, self.left, self.recv = right, left, recv
         self.a_send, self.a_recv, self.a_own = a_send, a_recv, a_own
@@ -189,32 +189,19 @@
             ).wait_recv()
 
 
-def is_near(halves):
-    gap = lax.axis_index("head") - lax.axis_index("ctx") // halves
-    return gap == 0
-
-
-def first_kernel(kv_ref, g_ref, all_ref, slots_ref, terms_ref, send, recv, own,
-                 right, left, z_recv, a_send, a_recv, a_own):
-    n, heads, halves = all_ref.shape[0], slots_ref.shape[0], slots_ref.shape[1]
+def first_kernel(kv_ref, g_ref, all_ref, slots_ref, send, recv, own, right, left, z_recv):
+    n, heads = all_ref.shape[0], slots_ref.shape[0]
     greet(n, heads)
     sp = Spread(
         lambda i, owner: g_ref if i == 0 else slots_ref.at[owner],
-        slots_ref, terms_ref, right, left, z_recv, a_send, a_recv, a_own,
+        slots_ref, None, right, left, z_recv, None, None, None,
     )
     g = Gather(kv_ref, all_ref, send, recv, own)
     g.start()
     sp.start_hop(1)
-    sp.hand_out(0)
     for j in range(1, g.half):
         g.forward(j)
     sp.arrive(1)
-
-    @pl.when(is_near(halves))
-    def _():
-        sp.wait_terms()
-
-    sp.end_hand_out(0)
     sp.end_hop(1)
     g.finish()
 
@@ -230,38 +217,32 @@
 
 def first_moves(kv, parts, n, heads):
     whole = pl.BlockSpec(memory_space=pl.ANY)
-    halves, padded, rows = parts.shape
     return pl.pallas_call(
         first_kernel,
         out_shape=[
             jax.ShapeDtypeStruct((n,) + kv.shape, kv.dtype),
             jax.ShapeDtypeStruct((heads,) + parts.shape, parts.dtype),
-            jax.ShapeDtypeStruct((n, padded, rows), parts.dtype),
         ],
         in_specs=[whole] * 2,
-        out_specs=[whole] * 3,
-        scratch_shapes=spread_sems(n, heads),
+        out_specs=[whole] * 2,
+        scratch_shapes=spread_sems(n, heads)[:6],
         compiler_params=pltpu.CompilerParams(collective_id=0, has_side_effects=True),
     )(kv, parts)
 
 
-def grad_kernel(low_ref, early_ref, near_ref, out_ref, att, slots, terms, copied, send, recv, own,
+def grad_kernel(low_ref, g_ref, early_ref, out_ref, att, slots, terms, send, recv, own,
                 right, left, z_recv, a_send, a_recv, a_own):
-    n, heads, halves = att.shape[0], slots.shape[0], slots.shape[1]
+    n, heads = att.shape[0], slots.shape[0]
     greet(n, heads)
     sp = Spread(
-        lambda i, owner: (early_ref if i <= 1 else slots).at[owner],
+        lambda i, owner: g_ref if i == 0 else (early_ref if i == 1 else slots).at[owner],
         slots, terms, right, left, z_recv, a_send, a_recv, a_own,
     )
     g = Gather(low_ref, att, send, recv, own)
-    near = is_near(halves)
     g.start()
     sp.start_hop(2)
+    sp.hand_out(0)
     sp.hand_out(1)
-
-    @pl.when(near)
-    def _():
-        pltpu.make_async_copy(near_ref, terms, copied).start()
 
     for i in range(1, max(heads - 1, g.half)):
         if i + 1 < heads:
@@ -272,16 +253,9 @@
         if i < g.half:
             g.forward(i)
 
-    @pl.when(near)
-    def _():
-        pltpu.make_async_copy(near_ref, terms, copied).wait()
-
-    for i in range(1, heads):
+    for i in range(heads):
         sp.end_hand_out(i)
-
-    @pl.when(jnp.logical_not(near))
-    def _():
-        sp.wait_terms()
+    sp.wait_terms()
 
     for i in range(2, heads):
         sp.end_hop(i)
@@ -295,9 +269,9 @@
         out_ref[...] += jnp.dot(terms[s], att[s], preferred_element_type=jnp.float32)[:count]
 
 
-def grad_product(low, early, near, count):
+def grad_product(low, parts, early, n, count):
     rows, width = low.shape
-    heads, n = early.shape[0], near.shape[0]
+    heads, _, padded, _ = early.shape
     whole = pl.BlockSpec(memory_space=pl.ANY)
     return pl.pallas_call(
         grad_kernel,
@@ -307,13 +281,12 @@
         scratch_shapes=[
             pltpu.VMEM((n, rows, width), low.dtype),
             pltpu.VMEM(early.shape, early.dtype),
-            pltpu.VMEM(near.shape, near.dtype),
-            pltpu.SemaphoreType.DMA,
+            pltpu.VMEM((n, padded, rows), early.dtype),
         ] + spread_sems(n, heads),
         compiler_params=pltpu.CompilerParams(
             collective_id=1, has_side_effects=True, vmem_limit_bytes=32 << 20,
         ),
-    )(low, early, near)
+    )(low, parts, early)
 
 
 def attend_kernel(pairs, lo_ref, hi_ref, slot_ref, q_ref, kv_ref, start_ref, pos_ref,
@@ -422,7 +395,7 @@
     count = grad_rows.shape[1] * heads // n
     parts = grad_rows.T.reshape(n // heads, count, tokens_local)
     parts = jnp.pad(parts, ((0, 0), (0, -count % 16), (0, 0)))
-    kv, early, near = first_moves(own_kv, parts, n, heads)
+    kv, early = first_moves(own_kv, parts, n, heads)
     kv = kv.reshape(n * tokens_local, -1)
 
     tile_count = tile_list.shape[0]
@@ -438,7 +411,7 @@
     attended, low = attend(
         queries, kv, lo, hi, slot, start.reshape(-1, 1), pos.reshape(-1, 1), kv_local, per_kv
     )
-    weight_grad = grad_product(low, early, near, count)
+    weight_grad = grad_product(low, parts, early, n, count)
     return (attended, weight_grad)
 
 

time: 92.8 us -> 79.1 us (0.85)
  the two profiles are of different devices: /device:TPU:3 before, /device:TPU:0 now
where the time goes in v5:
time: 79.1 us; the launch traced here: 79.2 us
  Pallas kernels  69.3 us (88%)
  local copies, waits for them, and re-layouts  6.43 us (8%)
  other arithmetic  2.73 us (3%)
    pallas_call x1, Pallas kernels, grad_product(): pl.pallas_call(grad_kernel, out_shape=jax.ShapeDtypeStruct((count, width)...  41.1 us
    pallas_call x1, Pallas kernels, first_moves(): pl.pallas_call(first_kernel, out_shape=[jax.ShapeDtypeStruct((n,) + kv.sh...  15.9 us
    pallas_call x1, Pallas kernels, attend(): pl.pallas_call(functools.partial(attend_kernel, pairs), grid_spec=pltpu.P...  12.3 us
    unnamed x11, local copies, waits for them, and re-layouts  2.35 us
    pad x1, local copies, waits for them, and re-layouts, on_device(): parts = jnp.pad(parts, ((0, 0), (0, -count % 16), (0, 0)))  1.75 us

profile of v5, /device:TPU:0, one launch (start us, length us, event | category | flops | bytes accessed | tf_op | source)
XLA Modules:
  0.0 79.2 jit_solution(1901668513311984676)
XLA Ops:
  0.6 0.0 copy-start
  0.6 0.0 copy-start.4
  0.7 0.8 %broadcast_multiply_fusion = (s32[2]{0:T(128)S(1)}, s32[2]{0:T(128)S(1)}) fusion(s32[16]{0:T(128)} %param.9, s32[]{:T(128)S(6)} %select_n.23), kind=kLoop, calls=%fused_computation.12 | loop fusion | flops 2 | bytes 28 | tf_op jit(solution)/shard_map/mul | solution.py:408
  1.5 1.3 %gather_fusion = s32[2,128]{1,0:T(2,128)S(1)} fusion(s32[16,128]{1,0:T(8,128)} %bitcast.9, s32[1024]{0:T(1024)S(1)} %pad_clamp_fusion), kind=kCustom, calls=%fused_computation | custom fusion | bytes 2056 | tf_op jit(solution)/shard_map/gather | solution.py:406
  2.7 1.0 %convert_reduce_fusion = s32[2,128]{1,0:T(2,128)S(1)} fusion(s32[2,128]{1,0:T(2,128)S(1)} %gather_fusion, s32[2048]{0:T(1024)} %param.8), kind=kLoop, calls=%fused_computation.1 | loop fusion | flops 1572608 | bytes 10240 | tf_op jit(solution)/shard_map/reduce_sum | solution.py:407
  3.8 0.1 slice_reduce_fusion
  3.9 0.8 select_reduce_fusion.slot_ref
  4.7 0.0 copy-done
  4.7 0.7 constant_dynamic-slice_fusion.kv_ref
  5.4 1.8 %pad.4.g_ref = bf16[2,368,256]{2,1,0:T(8,128)(2,1)} pad(bf16[2,360,256]{2,1,0:T(8,128)(2,1)} %bitcast.8, bf16[]{:T(256)} %constant.51.clone.1), padding=0_0x0_8x0_0 | pad | bytes 745474 | tf_op jit(solution)/shard_map/jit(_pad)/pad | solution.py:397
  7.2 15.9 %shard_map.68 = (bf16[8,256,256]{2,1,0:T(8,128)(2,1)}, bf16[4,2,368,256]{3,2,1,0:T(8,128)(2,1)}) custom-call(bf16[256,256]{1,0:T(8,128)(2,1)} %constant_dynamic-slice_fusion.kv_ref, bf16[2,368,256]{2,1,0:T(8,128)(2,1)} %pad.4.g_ref), custom_call_target="tpu_custom_call" | custom-call | tf_op jit(solution)/shard_map/pallas_call | solution.py:220
  23.1 0.1 copy.12.start_ref
  23.2 0.1 iota_add_fusion
  23.3 0.1 copy.13.pos_ref
  23.4 0.0 copy-done.4
  23.4 0.0 copy-start.3
  23.5 1.2 %copy-done.3 = bf16[8,256,256]{2,1,0:T(8,128)(2,1)S(1)} copy-done((bf16[8,256,256]{2,1,0:T(8,128)(2,1)S(1)}, bf16[8,256,256]{2,1,0:T(8,128)(2,1)}, u32[]{:S(2)}) %copy-start.3) | copy-done | bytes 1048600
  24.7 0.0 copy-start.1
  24.7 0.0 copy-start.2
  24.7 12.3 %shard_map.69 = (f32[256,1024]{1,0:T(8,128)}, bf16[256,1024]{1,0:T(8,128)(2,1)S(1)}) custom-call(s32[2]{0:T(128)S(1)} %and_select_fusion.lo_ref, s32[2]{0:T(128)S(1)} %get-tuple-element.11.hi_ref, s32[16]{0:T(128)S(1)} %select_reduce_fusion.slot_ref, bf16[256,1024]{1,0:T(8,128)(2,1)S(1)} %copy-done.4, bf16[2048,256]{1,0:T(8,128)(2,1)S(1)} %bitcast.7, ...), custom_call_target="tpu_custom_call" | custom-call | flops 536870912 | bytes 3145728 | tf_op jit(solution)/shard_map/pallas_call | solution.py:360
  37.0 0.0 copy-done.1
  37.0 0.0 copy-done.2
  37.0 41.1 %shard_map.70 = f32[360,1024]{1,0:T(8,128)S(1)} custom-call(bf16[256,1024]{1,0:T(8,128)(2,1)S(1)} %get-tuple-element.8.low_ref, bf16[2,368,256]{2,1,0:T(8,128)(2,1)S(1)} %copy-done.1, bf16[4,2,368,256]{3,2,1,0:T(8,128)(2,1)S(1)} %copy-done.2), custom_call_target="tpu_custom_call" | custom-call | tf_op jit(solution)/shard_map/pallas_call | solution.py:276
  78.1 1.1 %copy.15 = f32[360,1024]{1,0:T(8,128)} copy(f32[360,1024]{1,0:T(8,128)S(1)} %shard_map.70) | data formatting | bytes 2949120
  (3 shorter events, 0.0 us)
Async XLA Ops:
  0.6 4.1 %copy-start = (bf16[256,1024]{1,0:T(8,128)(2,1)S(1)}, bf16[256,1024]{1,0:T(8,128)(2,1)}, u32[]{:S(2)}) copy-start(bf16[256,1024]{1,0:T(8,128)(2,1)} %param.6) | copy-start | bytes 1572868
  0.6 22.8 %copy-start.4 = (bf16[256,1024]{1,0:T(8,128)(2,1)S(1)}, bf16[256,1024]{1,0:T(8,128)(2,1)}, u32[]{:S(2)}) copy-start(bf16[256,1024]{1,0:T(8,128)(2,1)} %q_ref.1) | copy-start | bytes 1572868
  23.4 1.2 %copy-start.3 = (bf16[8,256,256]{2,1,0:T(8,128)(2,1)S(1)}, bf16[8,256,256]{2,1,0:T(8,128)(2,1)}, u32[]{:S(2)}) copy-start(bf16[8,256,256]{2,1,0:T(8,128)(2,1)} %get-tuple-element.6) | copy-start | bytes 3145732
  24.7 12.3 %copy-start.1 = (bf16[2,368,256]{2,1,0:T(8,128)(2,1)S(1)}, bf16[2,368,256]{2,1,0:T(8,128)(2,1)}, u32[]{:S(2)}) copy-start(bf16[2,368,256]{2,1,0:T(8,128)(2,1)} %pad.4.g_ref) | copy-start | bytes 1130500
  24.7 12.3 %copy-start.2 = (bf16[4,2,368,256]{3,2,1,0:T(8,128)(2,1)S(1)}, bf16[4,2,368,256]{3,2,1,0:T(8,128)(2,1)}, u32[]{:S(2)}) copy-start(bf16[4,2,368,256]{3,2,1,0:T(8,128)(2,1)} %get-tuple-element.9.early_ref) | copy-start | bytes 4521988

commit v6 on v5

--- a/solution.py
+++ b/solution.py
@@ -245,12 +245,14 @@
     sp.hand_out(1)
 
     for i in range(1, max(heads - 1, g.half)):
+        if 1 < i < g.half:
+            g.forward(i)
         if i + 1 < heads:
             sp.arrive(i + 1)
             if i + 2 < heads:
                 sp.start_hop(i + 2)
             sp.hand_out(i + 1)
-        if i < g.half:
+        if i == 1 and i < g.half:
             g.forward(i)
 
     for i in range(heads):

time: 79.1 us -> 79.1 us (level)
    pallas_call x1, Pallas kernels: 12.3 us -> 11.1 us  [attend(): pl.pallas_call(functools.partial(attend_kernel, pairs), grid_spec=pltpu.P...]
where the time goes in v6:
time: 79.1 us; the launch traced here: 78.5 us
  Pallas kernels  68.7 us (87%)
  local copies, waits for them, and re-layouts  6.43 us (8%)
  other arithmetic  2.73 us (3%)
    pallas_call x1, Pallas kernels, grad_product(): pl.pallas_call(grad_kernel, out_shape=jax.ShapeDtypeStruct((count, width)...  41.7 us
    pallas_call x1, Pallas kernels, first_moves(): pl.pallas_call(first_kernel, out_shape=[jax.ShapeDtypeStruct((n,) + kv.sh...  15.9 us
    pallas_call x1, Pallas kernels, attend(): pl.pallas_call(functools.partial(attend_kernel, pairs), grid_spec=pltpu.P...  11.1 us
    unnamed x11, local copies, waits for them, and re-layouts  2.35 us
    pad x1, local copies, waits for them, and re-layouts, on_device(): parts = jnp.pad(parts, ((0, 0), (0, -count % 16), (0, 0)))  1.75 us

profile of v6, /device:TPU:0, one launch (start us, length us, event | category | flops | bytes accessed | tf_op | source)
XLA Modules:
  0.0 78.5 jit_solution(1529589469180612793)
XLA Ops:
  0.6 0.0 copy-start
  0.6 0.0 copy-start.4
  0.7 0.8 %broadcast_multiply_fusion = (s32[2]{0:T(128)S(1)}, s32[2]{0:T(128)S(1)}) fusion(s32[16]{0:T(128)} %param.9, s32[]{:T(128)S(6)} %select_n.23), kind=kLoop, calls=%fused_computation.12 | loop fusion | flops 2 | bytes 28 | tf_op jit(solution)/shard_map/mul | solution.py:410
  1.5 1.3 %gather_fusion = s32[2,128]{1,0:T(2,128)S(1)} fusion(s32[16,128]{1,0:T(8,128)} %bitcast.9, s32[1024]{0:T(1024)S(1)} %pad_clamp_fusion), kind=kCustom, calls=%fused_computation | custom fusion | bytes 2056 | tf_op jit(solution)/shard_map/gather | solution.py:408
  2.7 1.0 %convert_reduce_fusion = s32[2,128]{1,0:T(2,128)S(1)} fusion(s32[2,128]{1,0:T(2,128)S(1)} %gather_fusion, s32[2048]{0:T(1024)} %param.8), kind=kLoop, calls=%fused_computation.1 | loop fusion | flops 1572608 | bytes 10240 | tf_op jit(solution)/shard_map/reduce_sum | solution.py:409
  3.8 0.1 slice_reduce_fusion
  3.9 0.8 select_reduce_fusion.slot_ref
  4.7 0.0 copy-done
  4.7 0.7 constant_dynamic-slice_fusion.kv_ref
  5.4 1.8 %pad.4.g_ref = bf16[2,368,256]{2,1,0:T(8,128)(2,1)} pad(bf16[2,360,256]{2,1,0:T(8,128)(2,1)} %bitcast.8, bf16[]{:T(256)} %constant.51.clone.1), padding=0_0x0_8x0_0 | pad | bytes 745474 | tf_op jit(solution)/shard_map/jit(_pad)/pad | solution.py:399
  7.2 15.9 %shard_map.68 = (bf16[8,256,256]{2,1,0:T(8,128)(2,1)}, bf16[4,2,368,256]{3,2,1,0:T(8,128)(2,1)}) custom-call(bf16[256,256]{1,0:T(8,128)(2,1)} %constant_dynamic-slice_fusion.kv_ref, bf16[2,368,256]{2,1,0:T(8,128)(2,1)} %pad.4.g_ref), custom_call_target="tpu_custom_call" | custom-call | tf_op jit(solution)/shard_map/pallas_call | solution.py:220
  23.1 0.1 copy.12.start_ref
  23.2 0.1 iota_add_fusion
  23.3 0.1 copy.13.pos_ref
  23.4 0.0 copy-done.4
  23.4 0.0 copy-start.3
  23.5 1.2 %copy-done.3 = bf16[8,256,256]{2,1,0:T(8,128)(2,1)S(1)} copy-done((bf16[8,256,256]{2,1,0:T(8,128)(2,1)S(1)}, bf16[8,256,256]{2,1,0:T(8,128)(2,1)}, u32[]{:S(2)}) %copy-start.3) | copy-done | bytes 1048600
  24.7 0.0 copy-start.1
  24.7 0.0 copy-start.2
  24.7 11.1 %shard_map.69 = (f32[256,1024]{1,0:T(8,128)}, bf16[256,1024]{1,0:T(8,128)(2,1)S(1)}) custom-call(s32[2]{0:T(128)S(1)} %and_select_fusion.lo_ref, s32[2]{0:T(128)S(1)} %get-tuple-element.11.hi_ref, s32[16]{0:T(128)S(1)} %select_reduce_fusion.slot_ref, bf16[256,1024]{1,0:T(8,128)(2,1)S(1)} %copy-done.4, bf16[2048,256]{1,0:T(8,128)(2,1)S(1)} %bitcast.7, ...), custom_call_target="tpu_custom_call" | custom-call | flops 536870912 | bytes 3145728 | tf_op jit(solution)/shard_map/pallas_call | solution.py:362
  35.8 0.0 copy-done.1
  35.8 0.0 copy-done.2
  35.8 41.7 %shard_map.70 = f32[360,1024]{1,0:T(8,128)S(1)} custom-call(bf16[256,1024]{1,0:T(8,128)(2,1)S(1)} %get-tuple-element.8.low_ref, bf16[2,368,256]{2,1,0:T(8,128)(2,1)S(1)} %copy-done.1, bf16[4,2,368,256]{3,2,1,0:T(8,128)(2,1)S(1)} %copy-done.2), custom_call_target="tpu_custom_call" | custom-call | tf_op jit(solution)/shard_map/pallas_call | solution.py:278
  77.4 1.1 %copy.15 = f32[360,1024]{1,0:T(8,128)} copy(f32[360,1024]{1,0:T(8,128)S(1)} %shard_map.70) | data formatting | bytes 2949120
  (3 shorter events, 0.0 us)
Async XLA Ops:
  0.6 4.1 %copy-start = (bf16[256,1024]{1,0:T(8,128)(2,1)S(1)}, bf16[256,1024]{1,0:T(8,128)(2,1)}, u32[]{:S(2)}) copy-start(bf16[256,1024]{1,0:T(8,128)(2,1)} %param.6) | copy-start | bytes 1572868
  0.6 22.8 %copy-start.4 = (bf16[256,1024]{1,0:T(8,128)(2,1)S(1)}, bf16[256,1024]{1,0:T(8,128)(2,1)}, u32[]{:S(2)}) copy-start(bf16[256,1024]{1,0:T(8,128)(2,1)} %q_ref.1) | copy-start | bytes 1572868
  23.4 1.2 %copy-start.3 = (bf16[8,256,256]{2,1,0:T(8,128)(2,1)S(1)}, bf16[8,256,256]{2,1,0:T(8,128)(2,1)}, u32[]{:S(2)}) copy-start(bf16[8,256,256]{2,1,0:T(8,128)(2,1)} %get-tuple-element.6) | copy-start | bytes 3145732
  24.7 11.1 %copy-start.1 = (bf16[2,368,256]{2,1,0:T(8,128)(2,1)S(1)}, bf16[2,368,256]{2,1,0:T(8,128)(2,1)}, u32[]{:S(2)}) copy-start(bf16[2,368,256]{2,1,0:T(8,128)(2,1)} %pad.4.g_ref) | copy-start | bytes 1130500
  24.7 11.1 %copy-start.2 = (bf16[4,2,368,256]{3,2,1,0:T(8,128)(2,1)S(1)}, bf16[4,2,368,256]{3,2,1,0:T(8,128)(2,1)}, u32[]{:S(2)}) copy-start(bf16[4,2,368,256]{3,2,1,0:T(8,128)(2,1)} %get-tuple-element.9.early_ref) | copy-start | bytes 4521988
